TPU v7x, 512 devices: a whole 4x8x8 slice. The times are simulated.
512 devices in a mesh: section: 8 (over y_hi, core), dp: 64 (over y_lo, x, z).
Axes of the slice: x: 4, y: 8 (y_hi: 4, y_lo: 2; y = y_hi * 2 + y_lo), z: 8, core: 2. Of those that a mesh axis runs over, the one named last changes fastest.
Arguments:
- activations: bfloat16 [8, 16384, 2048], P('section', 'dp'), may hold values from -18 to 18
- norm_gain: bfloat16 [8, 2048], P('section'), may hold values from 0.099609375 to 1.8984375
- query_weight: bfloat16 [8, 2048, 2048], P('section', 'dp'), may hold values from -0.125 to 0.125
- keyval_weight: bfloat16 [8, 2048, 1024], P('section', 'dp'), may hold values from -0.25 to 0.25
- prefix_cache: bfloat16 [8, 32768, 1024], P('section', 'dp'), may hold values from -256 to 256
- random_blocks: int32 [128, 3], P('dp'), may hold values from 0 to 255, as said below
Outputs:
- section_output: bfloat16 [8, 16384, 2048], P('section', 'dp')
Inputs may be any that keep to these rules, and one draw needn't show every extreme that they name: `random_blocks`: for each query block q, 3 different cache blocks, all from (q // 2) * 4 to (q // 2 + 1) * 4 - 1.
All inputs are finite; a program needn't handle non-finite values.
Results may differ from a plain program's by a relative error of at most 0.0055.
The roundings to bfloat16 on the way count: a program that leaves them out, or rounds other values in their place, can miss the bound.
Values may be sent and summed in bfloat16 or wider, within the bound.
A program may use at most 64 MiB of HBM per device.

v0:
```python
import math

import jax
import jax.numpy as jnp
from jax import lax
from jax.sharding import PartitionSpec as P

H = 16
KVH = 4
HD = 128
BLK = 128
G = 2
R = 3


epsilon = 1e-05


def broadcast(block, axis, owner):
    block = jnp.where(lax.axis_index(axis) == owner, block, jnp.zeros_like(block))
    return lax.psum(block, axis)


def passed_along(shard, axis, by):
    peers = lax.axis_size(axis)
    pairs = [(i, i + by) for i in range(peers) if 0 <= i + by < peers]
    return lax.ppermute(shard, axis, pairs)


def passed_along_2(value, axis, steps):
    count = lax.axis_size(axis)
    pairs = [(source, (source + steps) % count) for source in range(count)]
    return lax.ppermute(value, axis, pairs)


def normalize(residual, gain):
    widened = residual.astype(jnp.float32)
    spread = jnp.mean(widened * widened, axis=-1, keepdims=True)
    return (widened * lax.rsqrt(spread + epsilon) * gain.astype(jnp.float32)).astype(jnp.bfloat16)


def visible(prior_valid):
    key_column = jnp.arange((G + R + 2) * BLK)[None, :]
    query_row = jnp.arange(BLK)[:, None]
    prior_start = (G + R) * BLK
    own_start = prior_start + BLK
    leading = key_column < prior_start
    prior_rows = (key_column >= prior_start) & (key_column < own_start) & prior_valid
    own_rows = (key_column >= own_start) & (key_column - own_start <= query_row)
    return leading | prior_rows | own_rows


def probabilities(scores, allowed):
    masked = jnp.where(allowed, scores, -jnp.inf)
    highest = jnp.max(masked, axis=-1, keepdims=True)
    raised = jnp.exp(masked - highest)
    return (raised / jnp.sum(raised, axis=-1, keepdims=True)).astype(jnp.bfloat16)


def per_device(activations, norm_gain, query_weight, keyval_weight, prefix_cache, random_blocks):
    residual = activations[0]
    tokens_here = residual.shape[0]
    block_count = tokens_here // BLK
    width = KVH * HD
    groups = H // KVH
    cache_rows = prefix_cache[0]
    stripe = cache_rows.shape[0] // BLK
    global_rows = broadcast(cache_rows[: G * BLK], "dp", 0)
    normed = normalize(residual, norm_gain[0])

    def add_rows(pieces):
        return jnp.dot(normed, pieces[0], preferred_element_type=jnp.float32)

    pieces = (
        lax.all_gather(query_weight, "dp", axis=1, tiled=True),
        lax.all_gather(keyval_weight, "dp", axis=1, tiled=True),
    )
    query_sums = add_rows(pieces[0])
    keyval_sums = add_rows(pieces[1])
    keyvals = keyval_sums.astype(jnp.bfloat16)
    last_block = passed_along(keyvals[tokens_here - BLK :], "dp", 1)
    own_blocks = keyvals.reshape(block_count, BLK, 2 * width)
    prior_blocks = jnp.concatenate([last_block[None], own_blocks[:-1]], axis=0)
    position = lax.axis_index("dp")
    local_ids = random_blocks - position * stripe
    cache_blocks = cache_rows.reshape(stripe, BLK, 2 * width)
    picked = jnp.take(cache_blocks, local_ids, axis=0).reshape(block_count, R * BLK, 2 * width)
    shared = jnp.broadcast_to(global_rows[None], (block_count, G * BLK, 2 * width))
    joined = jnp.concatenate([shared, picked, prior_blocks, own_blocks], axis=1)
    key_rows = joined[..., :width].reshape(block_count, -1, KVH, HD)
    value_rows = joined[..., width:].reshape(block_count, -1, KVH, HD)
    query_blocks = query_sums.astype(jnp.bfloat16).reshape(block_count, BLK, KVH, groups, HD)
    scores = jnp.einsum(
        "btkgd,bskd->bkgts", query_blocks, key_rows, preferred_element_type=jnp.float32
    ) / math.sqrt(HD)
    numbers = position * block_count + jnp.arange(block_count, dtype=jnp.int32)
    allowed = visible((numbers > 0)[:, None, None, None, None])
    probs = probabilities(scores, allowed)
    heads = jnp.einsum(
        "bkgts,bskd->btkgd", probs, value_rows, preferred_element_type=jnp.float32
    ).reshape(tokens_here, H * HD)
    summed = (residual.astype(jnp.float32) + heads).astype(jnp.bfloat16)
    result = passed_along_2(summed, "section", 1)
    return result[None]


def solution(mesh):
    return jax.shard_map(
        per_device,
        mesh=mesh,
        in_specs=(
            P("section", "dp", None),
            P("section", None),
            P("section", "dp", None),
            P("section", "dp", None),
            P("section", "dp", None),
            P("dp", None),
        ),
        out_specs=P("section", "dp", None),
        check_vma=False,
    )
```

profile of v0, /device:TPU:40, one launch (start us, length us, event | category | flops | bytes accessed | tf_op | source)
XLA Modules:
  0.0 1314.1 jit_solution(10151637308779851065)
XLA Ops:
  6.5 0.7 all-gather.3.cloned.1.call-update
  7.3 1.9 select_bitcast_fusion
  10.0 0.7 compare_and_fusion
  10.8 0.7 mul.42
  11.5 1.9 gather_fusion
  14.3 306.4 %all-gather.3.cloned.1.call-done = bf16[1,2048,1024]{2,1,0:T(8,128)(2,1)} async-done(((bf16[1,32,1024]{2,1,0:T(8,128)(2,1)}), bf16[1,2048,1024]{2,1,0:T(8,128)(2,1)}) %all-gather.3.cloned.1.call-update) | async-done | bytes 4194320 | tf_op jit(solution)/shard_map/all_gather | solution.py:76
  320.7 3.8 fusion.22
  324.6 2.8 collective-permute-start
  327.7 601.1 %all-reduce.2.cloned.1.call-done = bf16[256,1024]{1,0:T(8,128)(2,1)} async-done(((bf16[256,1024]{1,0:T(8,128)(2,1)}), bf16[256,1024]{1,0:T(8,128)(2,1)}) %all-reduce.2.cloned.1.call-update) | async-done | bytes 524304 | tf_op jit(solution)/shard_map/psum | solution.py:21
  928.8 1.2 broadcast_in_dim.54
  930.5 1.7 fusion.39
  932.1 3.7 copy.13
  935.8 2.4 copy.12
  938.2 305.9 %all-gather.5.cloned.1.call-done = bf16[1,2048,2048]{2,1,0:T(8,128)(2,1)} async-done(((bf16[1,32,2048]{2,1,0:T(8,128)(2,1)}), bf16[1,2048,2048]{2,1,0:T(8,128)(2,1)}) %all-gather.5.cloned.1.call-update) | async-done | bytes 8388624 | tf_op jit(solution)/shard_map/all_gather | solution.py:75
  1244.2 5.7 fusion.14
  1249.9 1.5 reshape.193
  1251.5 11.7 fusion.41
  1263.2 7.8 fusion.21
  1270.9 2.5 copy.17
  1273.4 1.9 reshape.194
  1275.3 1.9 fusion.18
  1277.2 1.9 collective-permute-start.1
  1279.1 27.5 %collective-permute-done.1 = bf16[256,2048]{1,0:T(8,128)(2,1)S(1)} collective-permute-done((bf16[256,2048]{1,0:T(8,128)(2,1)S(1)}, bf16[256,2048]{1,0:T(8,128)(2,1)S(1)}, u32[]{:S(2)}, u32[]{:S(2)}) %collective-permute-start.1) | collective-permute-done | bytes 1048608 | tf_op jit(solution)/shard_map/ppermute | solution.py:33
  1306.6 1.0 copy.40
  (28 shorter events, 2.7 us)
Async XLA Ops:
  6.5 6.9 copy-start
  6.5 314.2 %all-gather.3.cloned.1.call-start = ((), (), s32[]{:S(2)}) async-start(), calls=%async_computation.1 | async-start | bytes 4259840 | tf_op jit(solution)/shard_map/all_gather | solution.py:76
  7.3 921.5 %all-reduce.2.cloned.1.call-start = ((), (), s32[]{:S(2)}) async-start(), calls=%async_computation | async-start | bytes 1048576 | tf_op jit(solution)/shard_map/psum | solution.py:21
  9.2 1234.9 %all-gather.5.cloned.1.call-start = ((), (), s32[]{:S(2)}) async-start(), calls=%async_computation.2 | async-start | bytes 8519680 | tf_op jit(solution)/shard_map/all_gather | solution.py:75
  324.6 604.3 %collective-permute-start = (bf16[128,1024]{1,0:T(8,128)(2,1)S(1)}, bf16[128,1024]{1,0:T(8,128)(2,1)S(1)}, u32[]{:S(2)}, u32[]{:S(2)}) collective-permute-start(bf16[128,1024]{1,0:T(8,128)(2,1)S(1)} %get-tuple-element.9), channel_id=1, source_target_pairs={{0,1},{1,2},{2,3},{3,4},{4,5},{5,6},{6,7},{7,8},{8,9},{9,10},{10,1... | collective-permute-start | bytes 786440 | tf_op jit(solution)/shard_map/ppermute | solution.py:27
  932.1 312.0 %copy-start.1 = (bf16[1,256,2048]{2,1,0:T(8,128)(2,1)S(1)}, bf16[1,256,2048]{2,1,0:T(8,128)(2,1)}, u32[]{:S(2)}) copy-start(bf16[1,256,2048]{2,1,0:T(8,128)(2,1)} %param.6) | copy-start | bytes 3145732
  1251.5 11.7 copy-start.2
  1277.2 29.4 %collective-permute-start.1 = (bf16[256,2048]{1,0:T(8,128)(2,1)S(1)}, bf16[256,2048]{1,0:T(8,128)(2,1)S(1)}, u32[]{:S(2)}, u32[]{:S(2)}) collective-permute-start(bf16[256,2048]{1,0:T(8,128)(2,1)S(1)} %fusion.18), channel_id=1, source_target_pairs={{0,64},{64,128},{128,192},{192,256},{256,320},{320,384},{384,448},... | collective-permute-start | bytes 3145736 | tf_op jit(solution)/shard_map/ppermute | solution.py:33
Sparse Core Ops, SparseCore 0:
  9.4 311.2 all-gather.2
  323.6 605.1 all-reduce.1
  931.1 313.0 all-gather.4
where the time goes:
time: 1310 us
  waiting for transfers between devices  1240 us (95%)
  matrix products  29 us (2%)
  local copies, waits for them, and re-layouts  17.9 us (1%)
  between operations  13.3 us (1%)
    psum x1, waiting for transfers between devices, broadcast(): return lax.psum(block, axis)  601 us
    all_gather x1, waiting for transfers between devices, per_device(): lax.all_gather(keyval_weight, 'dp', axis=1, tiled=True)  306 us
    all_gather x1, waiting for transfers between devices, per_device(): lax.all_gather(query_weight, 'dp', axis=1, tiled=True)  306 us
    ppermute x1, waiting for transfers between devices, passed_along_2(): return lax.ppermute(value, axis, pairs)  27.5 us
  transfers between devices with their start and end apart: 5, of which 4 were waited for; matrix products, arithmetic and copies ran while one was open for 2% of the time, Pallas kernels for 0%

commit v1 on v0

v1 whole, which is shorter than its diff:
```python
import math

import jax
import jax.numpy as jnp
from jax import lax
from jax.experimental import pallas as pl
from jax.experimental.pallas import tpu as pltpu
from jax.sharding import PartitionSpec as P

KVH = 4
HD = 128
D = 2048
KVD = 512
TOK = 256
NX, NZ = 4, 8
ROWS = 32
EPS = 1e-05
MESH = pl.DeviceIdType.MESH
F32, BF16 = jnp.float32, jnp.bfloat16
SCALE = math.log2(math.e) / math.sqrt(HD)

PHASES = ((0, 512, 1024), (1024, 1280, 1536), (1536, 1792, 2048), (2048, 2304, 2560), (2560, 2816, 3072))
NP = len(PHASES)
NIN = 8


def kernel(
    act, gain, qw, kvw, cache, rb, out,
    W, G, res, nb, cbuf, kv, qb, ob, gown, gbuf, bown, bbuf,
    in_s, in_r, gs_s, gs_r, gx_s, gx_r, gz_s, gz_r, p1_s, p1_r, p2_s, p2_r, sib_s, sib_r, gsib_s, gsib_r,
    halo_s, halo_r, out_s, out_r,
):
    s, d = lax.axis_index("section"), lax.axis_index("dp")
    yh, c = lax.div(s, 2), lax.rem(s, 2)
    yl, xz = lax.div(d, 32), lax.rem(d, 32)
    x, z = lax.div(xz, NZ), lax.rem(xz, NZ)
    base = 32 * yl
    share, layer = 32 * c + xz, 2 * yh + yl
    swapped = c != yl

    def xat(k):
        return lax.rem(x + k + NX, NX)

    def zat(k):
        return lax.rem(z + k + NZ, NZ)

    def xdev(k):
        return (s, base + NZ * xat(k) + z)

    def zdev(k):
        return (s, base + NZ * x + zat(k))

    def worker(layer_, share_):
        return (2 * lax.div(layer_, 2) + lax.div(share_, 32), 32 * lax.rem(layer_, 2) + lax.rem(share_, 32))

    sibling = (2 * yh + 1 - c, d)
    partner = (2 * yh + 1 - c, 32 * (1 - yl) + xz)
    target = (lax.rem(layer + 1, 8), share)
    origin = worker(lax.rem(s + 7, 8), d)
    is_source = d == 0

    bar = pltpu.get_barrier_semaphore()

    def greet(dev):
        pl.semaphore_signal(bar, inc=1, device_id=dev, device_id_type=MESH)

    for dev in (xdev(1), xdev(-1), xdev(2), zdev(1), zdev(-1), sibling, origin):
        greet(dev)
    pl.when(swapped)(lambda: greet(partner))
    pl.when(share > 0)(lambda: greet(worker(layer, share - 1)))
    scattered = (x == 0) & jnp.logical_not((d == 0) & (c == 0))
    pl.when(scattered)(lambda: greet((layer, 0)))

    gown[...] = jnp.broadcast_to(gain[...].astype(F32), (8, D))
    blocks = lax.broadcasted_iota(jnp.int32, (8, 512), 1) // 128 + 4 * d
    row = lax.broadcasted_iota(jnp.int32, (8, 512), 0)
    picked = [
        (blocks == rb[b, 0]) | (blocks == rb[b, 1]) | (blocks == rb[b, 2]) for b in range(2)
    ]
    zero, never = jnp.zeros((8, 512), F32), jnp.full((8, 512), -jnp.inf, F32)
    bown[...] = jnp.where(row == 0, jnp.where(picked[0], zero, never), jnp.where(picked[1], zero, never))

    extra = jnp.where(is_source, 15 + c, 0)
    pl.semaphore_wait(bar, 7 + swapped.astype(jnp.int32) + (share < 63).astype(jnp.int32) + extra)

    sends = []

    def push(src, dst, send, recv, dev):
        copy = pltpu.make_async_remote_copy(src, dst, send, recv, device_id=dev, device_id_type=MESH)
        copy.start()
        sends.append(copy)

    def arrived(ref, sem):
        pltpu.make_async_copy(ref, ref, sem).wait()

    def entries(slot):
        return (
            (kvw.at[0], W.at[slot, x, z, :, 0:1024]),
            (qw.at[0], W.at[slot, x, z, :, 1024:3072]),
            (gown, gbuf),
            (act.at[0], res),
            (bown, bbuf),
            (cache.at[0, :, 0:256], cbuf.at[:, 0:256]),
            (cache.at[0, :, 512:768], cbuf.at[:, 512:768]),
            (cache.at[0, :, 256:512], cbuf.at[:, 256:512]),
            (cache.at[0, :, 768:1024], cbuf.at[:, 768:1024]),
        )

    def bring(first, last):
        def own():
            for k in range(first, last):
                src, dst = entries(yl)[k]
                pltpu.make_async_copy(src, dst, in_r.at[k]).start()

        def trade():
            for k in range(first, last):
                src, dst = entries(yl)[k]
                pltpu.make_async_remote_copy(
                    src, dst, in_s.at[k], in_r.at[k], device_id=partner, device_id_type=MESH
                ).start()

        pl.when(jnp.logical_not(swapped))(own)
        pl.when(swapped)(trade)

    def brought(k):
        arrived(entries(c)[k][1], in_r.at[k])

    def scatter_copy(ct, zt):
        return pltpu.make_async_remote_copy(
            cache.at[0, ROWS * zt : ROWS * zt + ROWS, 512 * ct : 512 * ct + 512], G.at[ct, zt],
            gs_s.at[8 * ct + zt], gs_r.at[0],
            device_id=(2 * yh + ct, 32 * c + zt), device_id_type=MESH,
        )

    def scatter(act_on):
        for ct in range(2):
            for zt in range(8):
                if (ct, zt) == (0, 0):
                    pl.when(c == 1)(lambda: act_on(scatter_copy(0, 0)))
                else:
                    act_on(scatter_copy(ct, zt))

    def globals_round():
        pl.when(x == 0)(lambda: arrived(G.at[c, z], gs_r.at[0]))

        def spread():
            for k in range(1, NX):
                pltpu.make_async_remote_copy(
                    G.at[c, z], G.at[c, z], gx_s.at[k - 1], gx_r.at[0], device_id=xdev(k), device_id_type=MESH
                ).start()

        pl.when(x == 0)(spread)
        yield
        pl.when(x != 0)(lambda: arrived(G.at[c, z], gx_r.at[0]))
        for k in range(4):
            a, b = (slice(0, 16), slice(16, 32)) if k == 3 else (slice(0, 32),) * 2
            push(G.at[c, zat(-k), a], G.at[c, zat(-k), a], gz_s.at[2 * k], gz_r.at[2 * k], zdev(1))
            push(G.at[c, zat(k), b], G.at[c, zat(k), b], gz_s.at[2 * k + 1], gz_r.at[2 * k + 1], zdev(-1))
            yield
            arrived(G.at[c, zat(-k - 1), a], gz_r.at[2 * k])
            arrived(G.at[c, zat(k + 1), b], gz_r.at[2 * k + 1])
        push(G.at[c], G.at[c], gsib_s.at[0], gsib_r.at[0], sibling)

    def x_then_z(p):
        cols = slice(PHASES[p][0], PHASES[p][1])
        mine = W.at[c, x, z, :, cols]
        for i, k in enumerate((1, -1, 2)):
            push(mine, mine, p1_s.at[p, i], p1_r.at[p, i], xdev(k))
        yield
        for i, k in enumerate((-1, 1, 2)):
            arrived(W.at[c, xat(k), z, :, cols], p1_r.at[p, i])
        for k in range(4):
            a, b = (slice(0, 2), slice(2, 4)) if k == 3 else (slice(0, 4),) * 2
            i = 3 + 2 * k
            src = W.at[c, a, zat(-k), :, cols]
            push(src, src, p1_s.at[p, i], p1_r.at[p, i], zdev(1))
            src = W.at[c, b, zat(k), :, cols]
            push(src, src, p1_s.at[p, i + 1], p1_r.at[p, i + 1], zdev(-1))
            yield
            arrived(W.at[c, a, zat(-k - 1), :, cols], p1_r.at[p, i])
            arrived(W.at[c, b, zat(k + 1), :, cols], p1_r.at[p, i + 1])

    def z_then_x(p):
        cols = slice(PHASES[p][1], PHASES[p][2])
        for k in range(4):
            a, b = (slice(0, 16), slice(16, 32)) if k == 3 else (slice(0, 32),) * 2
            i = 2 * k
            src = W.at[c, x, zat(-k), a, cols]
            push(src, src, p2_s.at[p, i], p2_r.at[p, i], zdev(1))
            src = W.at[c, x, zat(k), b, cols]
            push(src, src, p2_s.at[p, i + 1], p2_r.at[p, i + 1], zdev(-1))
            yield
            arrived(W.at[c, x, zat(-k - 1), a, cols], p2_r.at[p, i])
            arrived(W.at[c, x, zat(k + 1), b, cols], p2_r.at[p, i + 1])
        mine = W.at[c, x, :, :, cols]
        push(mine, mine, p2_s.at[p, 8], p2_r.at[p, 8], xdev(1))
        push(mine, mine, p2_s.at[p, 9], p2_r.at[p, 9], xdev(-1))
        yield
        arrived(W.at[c, xat(-1), :, :, cols], p2_r.at[p, 8])
        arrived(W.at[c, xat(1), :, :, cols], p2_r.at[p, 9])
        src = W.at[c, xat(-1), 0:4, :, cols]
        push(src, src, p2_s.at[p, 10], p2_r.at[p, 10], xdev(1))
        src = W.at[c, xat(1), 4:8, :, cols]
        push(src, src, p2_s.at[p, 11], p2_r.at[p, 11], xdev(-1))
        yield
        arrived(W.at[c, xat(2), 0:4, :, cols], p2_r.at[p, 10])
        arrived(W.at[c, xat(2), 4:8, :, cols], p2_r.at[p, 11])

    def share_half(p):
        half = W.at[c, :, :, :, PHASES[p][0] : PHASES[p][2]]
        push(half, half, sib_s.at[p], sib_r.at[p], sibling)

    def half_shared(p):
        arrived(W.at[1 - c, :, :, :, PHASES[p][0] : PHASES[p][2]], sib_r.at[p])

    def normalize():
        @pl.loop(0, TOK // 32)
        def _(i):
            rows = pl.ds(pl.multiple_of(i * 32, 32), 32)
            wide = res[rows, :].astype(F32)
            spread = jnp.mean(wide * wide, axis=-1, keepdims=True)
            nb[rows, :] = (wide * lax.rsqrt(spread + EPS) * gbuf[0:1, :]).astype(BF16)

    def project(first, columns, dst, row0):
        @pl.loop(0, columns // 256)
        def _(i):
            there = pl.ds(pl.multiple_of(first + i * 256, 256), 256)
            w = W[:, :, :, :, there].reshape(D, 256)
            y = jnp.dot(nb[...], w, preferred_element_type=F32)
            dst[row0 : row0 + TOK, pl.ds(pl.multiple_of(i * 256, 256), 256)] = y.astype(BF16)

    halo_to = worker(layer, share + 1)

    def halo_copy():
        return pltpu.make_async_remote_copy(
            kv.at[256:384], kv.at[0:128], halo_s.at[0], halo_r.at[0], device_id=halo_to, device_id_type=MESH
        )

    def keyvals():
        project(0, 1024, kv, 128)
        pl.when(share < 63)(lambda: halo_copy().start())

        def no_prior():
            kv[0:128, :] = jnp.zeros((128, 1024), BF16)

        pl.when(share == 0)(no_prior)

    def attend(j):
        project(1024 + 512 * j, 512, qb, 0)
        key = slice(HD * j, HD * j + HD)
        value = slice(KVD + HD * j, KVD + HD * j + HD)

        @pl.loop(0, 2)
        def _(i):
            b = 1 - i
            rows = pl.ds(pl.multiple_of(b * 128, 128), 128)
            near = pl.ds(pl.multiple_of(b * 128, 128), 256)
            q4 = jnp.concatenate([qb[rows, HD * g : HD * g + HD] for g in range(4)], axis=0)

            def score(keys):
                return SCALE * lax.dot_general(q4, keys, (((1,), (1,)), ((), ())), preferred_element_type=F32)

            s_glob = score(G[0, :, :, key].reshape(256, HD))
            s_rand = score(cbuf[:, key]) + bbuf[pl.ds(b, 1), :]
            at_row = lax.broadcasted_iota(jnp.int32, (512, 256), 0) % 128
            at_col = lax.broadcasted_iota(jnp.int32, (512, 256), 1)
            prior = (at_col < 128) & ((share > 0) | (b > 0))
            own = (at_col >= 128) & (at_col - 128 <= at_row)
            s_near = jnp.where(prior | own, score(kv[near, key]), -jnp.inf)
            top = jnp.maximum(
                jnp.max(s_rand, axis=-1, keepdims=True),
                jnp.max(jnp.maximum(s_glob, s_near), axis=-1, keepdims=True),
            )
            e_glob, e_rand, e_near = jnp.exp2(s_glob - top), jnp.exp2(s_rand - top), jnp.exp2(s_near - top)
            total = jnp.sum(e_rand, axis=-1, keepdims=True) + jnp.sum(e_glob + e_near, axis=-1, keepdims=True)
            heads = jnp.dot(e_glob.astype(BF16), G[1, :, :, key].reshape(256, HD), preferred_element_type=F32)
            heads += jnp.dot(e_rand.astype(BF16), cbuf[:, value], preferred_element_type=F32)
            heads += jnp.dot(e_near.astype(BF16), kv[near, value], preferred_element_type=F32)
            heads = heads / total
            for g in range(4):
                left = res[rows, 512 * j + HD * g : 512 * j + HD * g + HD].astype(F32)
                ob[j, rows, HD * g : HD * g + HD] = (left + heads[128 * g : 128 * g + 128]).astype(BF16)

        push(ob.at[j], out.at[0, :, 512 * j : 512 * j + 512], out_s.at[j], out_r.at[j], target)

    pl.when(is_source)(lambda: scatter(lambda copy: copy.start()))
    pl.when(is_source & (c == 0))(
        lambda: pltpu.make_async_copy(cache.at[0, 0:ROWS, 0:512], G.at[0, 0], gs_r.at[0]).start()
    )
    bring(0, 5)
    brought(0)
    active = [[x_then_z(0), z_then_x(0)]]
    waiting_globals = globals_round()
    done = []

    def tick():
        for p, group in enumerate(active):
            for process in list(group):
                if next(process, 0) == 0:
                    group.remove(process)
            if not group and p not in done:
                done.append(p)
                share_half(p)

    tick()
    bring(5, 9)
    brought(1)
    step = 0
    computed = 0
    globals_running = True
    while len(done) < NP:
        step += 1
        if step % 2 == 0 and len(active) < NP:
            p = len(active)
            active.append([x_then_z(p), z_then_x(p)])
        tick()
        if globals_running:
            globals_running = next(waiting_globals, 0) != 0
        if step == 7:
            brought(2)
            brought(3)
            normalize()
            half_shared(0)
            keyvals()
        if step >= 9 and step % 2 == 1 and computed < NP - 2:
            if computed == 0:
                brought(4)
                brought(5)
                brought(6)
                arrived(G.at[1 - c], gsib_r.at[0])
                pl.when(share > 0)(lambda: arrived(kv.at[0:128], halo_r.at[0]))
            if computed == 2:
                brought(7)
                brought(8)
            half_shared(computed + 1)
            attend(computed)
            computed += 1
    while computed < NP - 1:
        if computed == 2:
            brought(7)
            brought(8)
        half_shared(computed + 1)
        attend(computed)
        computed += 1

    for j in range(4):
        arrived(out.at[0, :, 512 * j : 512 * j + 512], out_r.at[j])
    for copy in sends:
        copy.wait_send()
    pl.when(share < 63)(lambda: halo_copy().wait_send())
    pl.when(is_source)(lambda: scatter(lambda copy: copy.wait_send()))

    def spread_sent():
        for k in range(1, NX):
            pltpu.make_async_remote_copy(
                G.at[c, z], G.at[c, z], gx_s.at[k - 1], gx_r.at[0], device_id=xdev(k), device_id_type=MESH
            ).wait_send()

    pl.when(x == 0)(spread_sent)

    def traded():
        for k in range(9):
            src, dst = entries(yl)[k]
            pltpu.make_async_remote_copy(
                src, dst, in_s.at[k], in_r.at[k], device_id=partner, device_id_type=MESH
            ).wait_send()

    pl.when(swapped)(traded)


def per_device(activations, norm_gain, query_weight, keyval_weight, prefix_cache, random_blocks):
    anywhere = pl.BlockSpec(memory_space=pl.ANY)
    dma = pltpu.SemaphoreType.DMA
    return pl.pallas_call(
        kernel,
        out_shape=jax.ShapeDtypeStruct((1, TOK, D), BF16),
        in_specs=[
            anywhere, pl.BlockSpec(memory_space=pltpu.VMEM), anywhere, anywhere, anywhere,
            pl.BlockSpec(memory_space=pltpu.SMEM),
        ],
        out_specs=anywhere,
        scratch_shapes=[
            pltpu.VMEM((2, NX, NZ, ROWS, 3072), BF16),
            pltpu.VMEM((2, NZ, ROWS, 512), BF16),
            pltpu.VMEM((TOK, D), BF16),
            pltpu.VMEM((TOK, D), BF16),
            pltpu.VMEM((512, 1024), BF16),
            pltpu.VMEM((384, 1024), BF16),
            pltpu.VMEM((TOK, 512), BF16),
            pltpu.VMEM((4, TOK, 512), BF16),
            pltpu.VMEM((8, D), F32),
            pltpu.VMEM((8, D), F32),
            pltpu.VMEM((8, 512), F32),
            pltpu.VMEM((8, 512), F32),
            dma((9,)), dma((9,)),
            dma((16,)), dma((1,)), dma((3,)), dma((1,)), dma((8,)), dma((8,)),
            dma((NP, 11)), dma((NP, 11)), dma((NP, 12)), dma((NP, 12)),
            dma((NP,)), dma((NP,)), dma((1,)), dma((1,)),
            dma((1,)), dma((1,)), dma((4,)), dma((4,)),
        ],
        compiler_params=pltpu.CompilerParams(
            collective_id=0, has_side_effects=True, vmem_limit_bytes=48 * 1024 * 1024
        ),
        cost_estimate=pl.CostEstimate(flops=5 * 10**9, bytes_accessed=2 * 10**7, transcendentals=4 * 10**6),
        name="relay_step",
    )(activations, norm_gain, query_weight, keyval_weight, prefix_cache, random_blocks)


def solution(mesh):
    return jax.shard_map(
        per_device,
        mesh=mesh,
        in_specs=(
            P("section", "dp", None),
            P("section", None),
            P("section", "dp", None),
            P("section", "dp", None),
            P("section", "dp", None),
            P("dp", None),
        ),
        out_specs=P("section", "dp", None),
        check_vma=False,
    )
```

time: 1310 us -> 116 us (0.09)
  the two profiles are of different devices: /device:TPU:40 before, /device:TPU:8 now
where the time goes in v1:
time: 116 us; the launch traced here: 115 us
  Pallas kernels  109 us (94%)
  local copies, waits for them, and re-layouts  6.54 us (6%)
    pallas_call x1, Pallas kernels, per_device(): pl.pallas_call(kernel, out_shape=jax.ShapeDtypeStruct((1, TOK, D), BF16),...  109 us
    unnamed x13, local copies, waits for them, and re-layouts  6.54 us

profile of v1, /device:TPU:8, one launch (start us, length us, event | category | flops | bytes accessed | tf_op | source)
XLA Modules:
  0.0 115.3 jit_solution(14289496609440749120)
XLA Ops:
  0.0 0.0 copy-start
  0.0 1.2 %copy-done = bf16[1,256,2048]{2,1,0:T(8,128)(2,1)S(1)} copy-done((bf16[1,256,2048]{2,1,0:T(8,128)(2,1)S(1)}, bf16[1,256,2048]{2,1,0:T(8,128)(2,1)}, u32[]{:S(2)}) %copy-start) | copy-done | bytes 1048600
  1.2 0.0 copy-start.1
  1.2 1.2 %copy-done.1 = bf16[1,512,1024]{2,1,0:T(8,128)(2,1)S(1)} copy-done((bf16[1,512,1024]{2,1,0:T(8,128)(2,1)S(1)}, bf16[1,512,1024]{2,1,0:T(8,128)(2,1)}, u32[]{:S(2)}) %copy-start.1) | copy-done | bytes 1048600
  2.5 0.0 copy-start.2
  2.5 0.9 copy-done.2
  3.4 0.0 copy-start.3
  3.4 0.8 copy-done.3
  4.2 0.0 copy-start.4
  4.2 0.7 copy-done.4
  4.9 0.0 copy-start.5
  4.9 0.7 copy-done.5
  5.6 108.7 %relay_step.1 = bf16[1,256,2048]{2,1,0:T(8,128)(2,1)S(1)} custom-call(bf16[1,256,2048]{2,1,0:T(8,128)(2,1)S(1)} %copy-done, bf16[1,2048]{1,0:T(2,128)(2,1)S(1)} %copy-done.4, bf16[1,32,2048]{2,1,0:T(8,128)(2,1)S(1)} %copy-done.2, bf16[1,32,1024]{2,1,0:T(8,128)(2,1)S(1)} %copy-done.3, bf16[1,512,1024]{2,1,0:T(8,128)(2,1)S(1)} %copy-done.1, s32[2,3]{1,0:T(2,128)S(1)} %copy-done.5), custom_call_target="tpu_custom_call" | custom-call | flops 5000000000 | bytes 20000000 | tf_op jit(solution)/shard_map/relay_step/pallas_call | solution.py:374
  114.3 1.0 copy.8
Async XLA Ops:
  0.0 1.2 %copy-start = (bf16[1,256,2048]{2,1,0:T(8,128)(2,1)S(1)}, bf16[1,256,2048]{2,1,0:T(8,128)(2,1)}, u32[]{:S(2)}) copy-start(bf16[1,256,2048]{2,1,0:T(8,128)(2,1)} %act.1) | copy-start | bytes 3145732
  1.2 1.2 %copy-start.1 = (bf16[1,512,1024]{2,1,0:T(8,128)(2,1)S(1)}, bf16[1,512,1024]{2,1,0:T(8,128)(2,1)}, u32[]{:S(2)}) copy-start(bf16[1,512,1024]{2,1,0:T(8,128)(2,1)} %cache.1) | copy-start | bytes 3145732
  2.5 0.9 copy-start.2
  3.4 0.8 copy-start.3
  4.2 0.7 copy-start.4
  4.9 0.7 copy-start.5

commit v2 on v0

v2 whole, which is shorter than its diff:
```python
import math

import jax
import jax.numpy as jnp
from jax import lax
from jax.experimental import pallas as pl
from jax.experimental.pallas import tpu as pltpu
from jax.sharding import PartitionSpec as P

KVH = 4
HD = 128
D = 2048
KVD = 512
TOK = 256
NX, NZ = 4, 8
ROWS = 32
EPS = 1e-05
MESH = pl.DeviceIdType.MESH
F32, BF16 = jnp.float32, jnp.bfloat16
SCALE = math.log2(math.e) / math.sqrt(HD)

GROUP = 768
SPLIT = (256, 256, 256, 128)
NTOKENS = 245
ORDER = (
    ("A", 0, 0), ("B", 0, 0), ("A", 1, 0), ("B", 1, 0), ("U", 0, 0), ("B", 0, 1), ("c", 0, 0), ("A", 0, 1),
    ("F", 0, 0), ("B", 1, 1), ("A", 1, 1), ("F", 1, 0), ("B", 0, 2), ("A", 0, 2), ("U", 0, 1), ("B", 1, 2),
    ("F", 0, 1), ("A", 2, 0), ("A", 1, 2), ("B", 2, 0), ("B", 0, 3), ("F", 1, 1), ("F", 0, 2), ("A", 0, 3),
    ("n", 0, 0), ("U", 0, 2), ("B", 1, 3), ("A", 1, 3), ("F", 1, 2), ("A", 2, 1), ("B", 0, 4), ("B", 2, 1),
    ("F", 0, 3), ("A", 0, 4), ("F", 2, 0), ("U", 0, 3), ("B", 1, 4), ("F", 1, 3), ("A", 1, 4), ("A", 3, 0),
    ("B", 3, 0), ("F", 0, 4), ("G", 0, 0), ("A", 2, 2), ("A", 0, 5), ("B", 2, 2), ("U", 0, 4), ("F", 2, 1),
    ("A", 1, 5), ("F", 1, 4), ("G", 1, 0), ("B", 3, 1), ("A", 3, 1), ("F", 3, 0), ("G", 0, 1), ("A", 2, 3),
    ("B", 2, 3), ("U", 0, 5), ("F", 2, 2), ("G", 1, 1), ("B", 3, 2), ("q", 0, 0), ("A", 2, 4), ("B", 2, 4),
    ("F", 2, 3), ("A", 3, 2), ("F", 3, 1), ("B", 3, 3), ("q", 1, 0), ("F", 3, 2), ("F", 2, 4), ("A", 2, 5),
    ("G", 2, 0), ("A", 3, 3), ("B", 3, 4), ("t", 0, 1), ("F", 3, 3), ("t", 0, 0), ("G", 2, 1), ("A", 3, 4),
    ("F", 3, 4), ("G", 3, 0), ("t", 1, 1), ("q", 2, 0), ("A", 3, 5), ("G", 3, 1), ("t", 1, 0), ("t", 2, 1),
    ("q", 3, 0), ("t", 2, 0), ("t", 3, 1), ("t", 3, 0),
)


def kernel(
    act, gain, qw, kvw, cache, rb, out,
    W, G, res, nb, cbuf, kv, qb, ob, gown, gbuf, bown, bbuf,
    in_s, in_r, gs_s, gs_r, gx_s, gx_r, all_s, all_r,
):
    s, d = lax.axis_index("section"), lax.axis_index("dp")
    yh, c = lax.div(s, 2), lax.rem(s, 2)
    yl, xz = lax.div(d, 32), lax.rem(d, 32)
    x, z = lax.div(xz, NZ), lax.rem(xz, NZ)
    base = 32 * yl
    share, layer = 32 * c + xz, 2 * yh + yl
    swapped = c != yl

    def xat(k):
        return lax.rem(x + k + NX, NX)

    def zat(k):
        return lax.rem(z + k + NZ, NZ)

    def xdev(k):
        return (s, base + NZ * xat(k) + z)

    def zdev(k):
        return (s, base + NZ * x + zat(k))

    def worker(layer_, share_):
        return (2 * lax.div(layer_, 2) + lax.div(share_, 32), 32 * lax.rem(layer_, 2) + lax.rem(share_, 32))

    sibling = (2 * yh + 1 - c, d)
    partner = (2 * yh + 1 - c, 32 * (1 - yl) + xz)
    target = (lax.rem(layer + 1, 8), share)
    origin = worker(lax.rem(s + 7, 8), d)
    is_source = d == 0

    bar = pltpu.get_barrier_semaphore()

    def greet(dev):
        pl.semaphore_signal(bar, inc=1, device_id=dev, device_id_type=MESH)

    for dev in (xdev(1), xdev(-1), xdev(2), zdev(1), zdev(-1), sibling, origin):
        greet(dev)
    pl.when(swapped)(lambda: greet(partner))
    pl.when(share > 0)(lambda: greet(worker(layer, share - 1)))
    scattered = (x == 0) & jnp.logical_not((d == 0) & (c == 0))
    pl.when(scattered)(lambda: greet((layer, 0)))

    gown[...] = jnp.broadcast_to(gain[...].astype(F32), (8, D))
    blocks = lax.broadcasted_iota(jnp.int32, (8, 512), 1) // 128 + 4 * d
    row = lax.broadcasted_iota(jnp.int32, (8, 512), 0)
    picked = [
        (blocks == rb[b, 0]) | (blocks == rb[b, 1]) | (blocks == rb[b, 2]) for b in range(2)
    ]
    zero, never = jnp.zeros((8, 512), F32), jnp.full((8, 512), -jnp.inf, F32)
    bown[...] = jnp.where(row == 0, jnp.where(picked[0], zero, never), jnp.where(picked[1], zero, never))

    extra = jnp.where(is_source, 15 + c, 0)
    pl.semaphore_wait(bar, 7 + swapped.astype(jnp.int32) + (share < 63).astype(jnp.int32) + extra)

    sends, tokens, seen = [], {}, set()

    def push(token, src, dev, recv=None, dst=None):
        i = len(tokens)
        tokens[token] = (src if recv is None else recv, i)
        copy = pltpu.make_async_remote_copy(
            src, src if dst is None else dst, all_s.at[i], all_r.at[i], device_id=dev, device_id_type=MESH
        )
        copy.start()
        sends.append(copy)

    def arrived(ref, sem):
        pltpu.make_async_copy(ref, ref, sem).wait()

    def await_token(*names):
        for name in names:
            if name not in seen:
                seen.add(name)
                ref, i = tokens[name]
                arrived(ref, all_r.at[i])

    def entries(slot):
        pairs = []
        for j in range(KVH):
            at = GROUP * j
            for src, first, last in (
                (kvw.at[0, :, HD * j : HD * j + HD], at, at + 128),
                (kvw.at[0, :, KVD + HD * j : KVD + HD * j + HD], at + 128, at + 256),
                (qw.at[0, :, 512 * j : 512 * j + 512], at + 256, at + 768),
            ):
                pairs.append((src, W.at[slot, x, z, :, first:last]))
        pairs += [(gown, gbuf), (act.at[0], res), (bown, bbuf)]
        for j in range(KVH):
            for h in range(2):
                first = KVD * h + HD * j
                pairs.append((cache.at[0, :, first : first + HD], cbuf.at[j, h]))
        return pairs

    def trade_copy(k):
        src, dst = entries(yl)[k]
        return pltpu.make_async_remote_copy(
            src, dst, in_s.at[k], in_r.at[k], device_id=partner, device_id_type=MESH
        )

    def bring(first, last):
        def own():
            for k in range(first, last):
                src, dst = entries(yl)[k]
                pltpu.make_async_copy(src, dst, in_r.at[k]).start()

        def trade():
            for k in range(first, last):
                trade_copy(k).start()

        pl.when(jnp.logical_not(swapped))(own)
        pl.when(swapped)(trade)

    def brought(*which):
        for k in which:
            if k not in seen:
                seen.add(k)
                arrived(entries(c)[k][1], in_r.at[k])

    def scatter_copy(ct, zt):
        return pltpu.make_async_remote_copy(
            cache.at[0, ROWS * zt : ROWS * zt + ROWS, 512 * ct : 512 * ct + 512], G.at[ct, zt],
            gs_s.at[8 * ct + zt], gs_r.at[0],
            device_id=(2 * yh + ct, 32 * c + zt), device_id_type=MESH,
        )

    def scatter(act_on):
        for ct in range(2):
            for zt in range(8):
                if (ct, zt) == (0, 0):
                    pl.when(c == 1)(lambda: act_on(scatter_copy(0, 0)))
                else:
                    act_on(scatter_copy(ct, zt))

    def spread_copy(k):
        return pltpu.make_async_remote_copy(
            G.at[c, z], G.at[c, z], gx_s.at[k - 1], gx_r.at[0], device_id=xdev(k), device_id_type=MESH
        )

    def spread(act_on):
        for k in range(1, NX):
            act_on(spread_copy(k))

    def halves(k, size):
        return (slice(0, size // 2), slice(size // 2, size)) if k == 3 else (slice(0, size),) * 2

    def ring(tag, k, block, size):
        a, b = halves(k, size)
        push((tag, "r", k + 1), block(zat(-k), a), zdev(1), block(zat(-k - 1), a))
        push((tag, "l", k + 1), block(zat(k), b), zdev(-1), block(zat(k + 1), b))

    def step_u(_, k):
        def block(at, part):
            return G.at[c, at, part]

        if k == 0:
            pl.when(x == 0)(lambda: arrived(G.at[c, z], gs_r.at[0]))
            pl.when(x == 0)(lambda: spread(lambda copy: copy.start()))
            return
        k -= 1
        if k == 0:
            pl.when(x != 0)(lambda: arrived(G.at[c, z], gx_r.at[0]))
        else:
            await_token(("U", "r", k), ("U", "l", k))
        if k < 4:
            ring("U", k, block, 32)
        else:
            push("Us", G.at[c], sibling, G.at[1 - c])

    def columns_a(p):
        return slice(GROUP * p, GROUP * p + SPLIT[p])

    def columns_b(p):
        return slice(GROUP * p + SPLIT[p], GROUP * (p + 1))

    def offsets(k):
        return (0,) if k == 0 else (4,) if k == 4 else (-k, k)

    def step_a(p, k):
        cols = columns_a(p)

        def block(at, part):
            return W.at[c, part, at, :, cols]

        if k == 0:
            brought(3 * p, 3 * p + 1, 3 * p + 2)
            for i in (1, -1, 2):
                push(("A", p, "x", i), W.at[c, x, z, :, cols], xdev(i), W.at[c, xat(-i), z, :, cols])
            return
        k -= 1
        if k == 0:
            await_token(*(("A", p, "x", i) for i in (1, -1, 2)))
        else:
            await_token((("A", p), "r", k), (("A", p), "l", k))
        if k < 4:
            ring(("A", p), k, block, 4)
        for q in offsets(k):
            push(("A", p, "s", q), W.at[c, :, zat(q), :, cols], sibling, W.at[1 - c, :, zat(q), :, cols])

    def hand_b(p, i, xo):
        cols = columns_b(p)
        push(("B", p, "s", i), W.at[c, xat(xo), :, :, cols], sibling, W.at[1 - c, xat(xo), :, :, cols])

    def step_b(p, k):
        cols = columns_b(p)

        def block(at, part):
            return W.at[c, x, at, part, cols]

        if k == 0:
            brought(3 * p, 3 * p + 1, 3 * p + 2)
        else:
            await_token((("B", p), "r", k), (("B", p), "l", k))
        if k < 4:
            ring(("B", p), k, block, 32)
        for q in offsets(k):
            mine = W.at[c, x, zat(q), :, cols]
            push(("B", p, "a", q), mine, xdev(1), W.at[c, xat(-1), zat(q), :, cols])
            push(("B", p, "b", q), mine, xdev(-1), W.at[c, xat(1), zat(q), :, cols])
        if k == 4:
            hand_b(p, 0, 0)

    def step_f(p, k):
        cols = columns_b(p)

        def along(xo, q, part):
            return W.at[c, xat(xo), zat(q), part, cols]

        await_token(*(("B", p, way, q) for way in "ab" for q in offsets(k)))
        if k in (0, 4):
            up, down, qa, qb_ = slice(0, 16), slice(16, 32), k, k
        else:
            up, down, qa, qb_ = slice(0, 32), slice(0, 32), -k, k
        push(("F", p, "a", k), along(-1, qa, up), xdev(1), along(2, qa, up))
        push(("F", p, "b", k), along(1, qb_, down), xdev(-1), along(2, qb_, down))

    def step_g(p, k):
        if k == 0:
            await_token(*(("B", p, way, q) for way in "ab" for q in range(-3, 5)))
            hand_b(p, 1, -1)
            hand_b(p, 2, 1)
        else:
            await_token(*(("F", p, way, q) for way in "ab" for q in range(5)))
            hand_b(p, 3, 2)

    def half_shared(p):
        if SPLIT[p]:
            await_token(*(("A", p, "s", q) for q in range(-3, 5)))
        if SPLIT[p] < GROUP:
            await_token(*(("B", p, "s", i) for i in range(4)))

    def step_c(*_):
        bring(15, 23)

    def step_n(*_):
        brought(12, 13)

        @pl.loop(0, TOK // 32)
        def _(i):
            rows = pl.ds(pl.multiple_of(i * 32, 32), 32)
            wide = res[rows, :].astype(F32)
            spread_ = jnp.mean(wide * wide, axis=-1, keepdims=True)
            nb[rows, :] = (wide * lax.rsqrt(spread_ + EPS) * gbuf[0:1, :]).astype(BF16)

    halo_to = worker(layer, share + 1)

    def halo_copy(j):
        cols = slice(256 * j, 256 * j + 256)
        return pltpu.make_async_remote_copy(
            kv.at[256:384, cols], kv.at[0:128, cols], in_s.at[23 + j], in_r.at[23 + j],
            device_id=halo_to, device_id_type=MESH,
        )

    def step_q(j, _):
        half_shared(j)

        def times(first):
            w = W[:, :, :, :, GROUP * j + first : GROUP * j + first + 256].reshape(D, 256)
            return jnp.dot(nb[...], w, preferred_element_type=F32).astype(BF16)

        kv[128:384, 256 * j : 256 * j + 256] = times(0)
        pl.when(share < 63)(lambda: halo_copy(j).start())
        qb[j, :, 0:256] = times(256)
        qb[j, :, 256:512] = times(512)

    def step_t(j, b):
        brought(14, 15 + 2 * j, 16 + 2 * j)
        await_token("Us")
        if b == 0:
            pl.when(share > 0)(lambda: arrived(kv.at[0:128, 256 * j : 256 * j + 256], in_r.at[23 + j]))
        key = slice(HD * j, HD * j + HD)
        rows = slice(128 * b, 128 * b + 128)
        near = slice(128 * b, 128 * b + 256)
        near_key, near_value = slice(256 * j, 256 * j + 128), slice(256 * j + 128, 256 * j + 256)
        q4 = jnp.concatenate([qb[j, rows, HD * g : HD * g + HD] for g in range(4)], axis=0)

        def score(keys):
            return SCALE * lax.dot_general(q4, keys, (((1,), (1,)), ((), ())), preferred_element_type=F32)

        s_glob = score(G[0, :, :, key].reshape(256, HD))
        s_rand = score(cbuf[j, 0]) + bbuf[b : b + 1, :]
        at_row = lax.broadcasted_iota(jnp.int32, (512, 256), 0) % 128
        at_col = lax.broadcasted_iota(jnp.int32, (512, 256), 1)
        prior = at_col < 128
        if b == 0:
            prior = prior & (share > 0)
        own = (at_col >= 128) & (at_col - 128 <= at_row)
        s_near = jnp.where(prior | own, score(kv[near, near_key]), -jnp.inf)
        top = jnp.maximum(
            jnp.max(s_rand, axis=-1, keepdims=True),
            jnp.max(jnp.maximum(s_glob, s_near), axis=-1, keepdims=True),
        )
        e_glob, e_rand, e_near = jnp.exp2(s_glob - top), jnp.exp2(s_rand - top), jnp.exp2(s_near - top)
        total = jnp.sum(e_rand, axis=-1, keepdims=True) + jnp.sum(e_glob + e_near, axis=-1, keepdims=True)
        heads = jnp.dot(e_glob.astype(BF16), G[1, :, :, key].reshape(256, HD), preferred_element_type=F32)
        heads += jnp.dot(e_rand.astype(BF16), cbuf[j, 1], preferred_element_type=F32)
        heads += jnp.dot(e_near.astype(BF16), kv[near, near_value], preferred_element_type=F32)
        heads = heads / total
        for g in range(4):
            left = res[rows, 512 * j + HD * g : 512 * j + HD * g + HD].astype(F32)
            ob[j, rows, HD * g : HD * g + HD] = (left + heads[128 * g : 128 * g + 128]).astype(BF16)
        there = out.at[0, rows, 512 * j : 512 * j + 512]
        push(("o", j, b), ob.at[j, rows], target, there, there)

    pl.when(is_source)(lambda: scatter(lambda copy: copy.start()))
    pl.when(is_source & (c == 0))(
        lambda: pltpu.make_async_copy(cache.at[0, 0:ROWS, 0:512], G.at[0, 0], gs_r.at[0]).start()
    )
    bring(0, 15)

    def no_prior():
        kv[0:128, :] = jnp.zeros((128, 1024), BF16)

    pl.when(share == 0)(no_prior)
    steps = dict(
        A=step_a, B=step_b, F=step_f, G=step_g, U=step_u, c=step_c, n=step_n, q=step_q, t=step_t
    )
    for name, p, k in ORDER:
        steps[name](p, k)

    await_token(*(("o", j, b) for j in range(KVH) for b in range(2)))
    for copy in sends:
        copy.wait_send()
    for j in range(KVH):
        pl.when(share < 63)(lambda j=j: halo_copy(j).wait_send())
    pl.when(is_source)(lambda: scatter(lambda copy: copy.wait_send()))
    pl.when(x == 0)(lambda: spread(lambda copy: copy.wait_send()))

    def traded():
        for k in range(23):
            trade_copy(k).wait_send()

    pl.when(swapped)(traded)


def per_device(activations, norm_gain, query_weight, keyval_weight, prefix_cache, random_blocks):
    anywhere = pl.BlockSpec(memory_space=pl.ANY)
    dma = pltpu.SemaphoreType.DMA
    return pl.pallas_call(
        kernel,
        out_shape=jax.ShapeDtypeStruct((1, TOK, D), BF16),
        in_specs=[
            anywhere, pl.BlockSpec(memory_space=pltpu.VMEM), anywhere, anywhere, anywhere,
            pl.BlockSpec(memory_space=pltpu.SMEM),
        ],
        out_specs=anywhere,
        scratch_shapes=[
            pltpu.VMEM((2, NX, NZ, ROWS, 3072), BF16),
            pltpu.VMEM((2, NZ, ROWS, 512), BF16),
            pltpu.VMEM((TOK, D), BF16),
            pltpu.VMEM((TOK, D), BF16),
            pltpu.VMEM((4, 2, 512, HD), BF16),
            pltpu.VMEM((384, 1024), BF16),
            pltpu.VMEM((4, TOK, 512), BF16),
            pltpu.VMEM((4, TOK, 512), BF16),
            pltpu.VMEM((8, D), F32),
            pltpu.VMEM((8, D), F32),
            pltpu.VMEM((8, 512), F32),
            pltpu.VMEM((8, 512), F32),
            dma((27,)), dma((27,)),
            dma((16,)), dma((1,)), dma((3,)), dma((1,)), dma((NTOKENS,)), dma((NTOKENS,)),
        ],
        compiler_params=pltpu.CompilerParams(
            collective_id=0, has_side_effects=True, vmem_limit_bytes=60 * 1024 * 1024
        ),
        cost_estimate=pl.CostEstimate(flops=5 * 10**9, bytes_accessed=2 * 10**7, transcendentals=4 * 10**6),
        name="relay_step",
    )(activations, norm_gain, query_weight, keyval_weight, prefix_cache, random_blocks)


def solution(mesh):
    return jax.shard_map(
        per_device,
        mesh=mesh,
        in_specs=(
            P("section", "dp", None),
            P("section", None),
            P("section", "dp", None),
            P("section", "dp", None),
            P("section", "dp", None),
            P("dp", None),
        ),
        out_specs=P("section", "dp", None),
        check_vma=False,
    )
```

time: 1310 us -> 91.8 us (0.07)
  the two profiles are of different devices: /device:TPU:40 before, /device:TPU:2 now
where the time goes in v2:
time: 91.8 us; the launch traced here: 91.6 us
  Pallas kernels  89.2 us (97%)
  local copies, waits for them, and re-layouts  2.3 us (3%)
    pallas_call x1, Pallas kernels, per_device(): pl.pallas_call(kernel, out_shape=jax.ShapeDtypeStruct((1, TOK, D), BF16),...  89.2 us
    unnamed x1, local copies, waits for them, and re-layouts  2.3 us

profile of v2, /device:TPU:2, one launch (start us, length us, event | category | flops | bytes accessed | tf_op | source)
XLA Modules:
  0.0 91.6 jit_solution(17753564075444999312)
XLA Ops:
  0.0 89.2 %relay_step.1 = bf16[1,256,2048]{2,1,0:T(8,128)(2,1)} custom-call(bf16[1,256,2048]{2,1,0:T(8,128)(2,1)} %act.1, bf16[1,2048]{1,0:T(2,128)(2,1)} %gain.1, bf16[1,32,2048]{2,1,0:T(8,128)(2,1)} %qw.1, bf16[1,32,1024]{2,1,0:T(8,128)(2,1)} %kvw.1, bf16[1,512,1024]{2,1,0:T(8,128)(2,1)} %cache.1, s32[2,3]{1,0:T(2,128)} %rb.1), custom_call_target="tpu_custom_call" | custom-call | flops 5000000000 | bytes 20000000 | tf_op jit(solution)/shard_map/relay_step/pallas_call | solution.py:401
  89.2 2.3 %copy.8 = bf16[1,256,2048]{2,1,0:T(8,128)(2,1)} copy(bf16[1,256,2048]{2,1,0:T(8,128)(2,1)} %relay_step.1) | data formatting | bytes 2097152

commit v3 on v2

--- a/solution.py
+++ b/solution.py
@@ -20,21 +20,21 @@
 SCALE = math.log2(math.e) / math.sqrt(HD)
 
 GROUP = 768
-SPLIT = (256, 256, 256, 128)
-NTOKENS = 245
+SPLIT = (256, 256, 384, 128)
+NTOKENS = 217
 ORDER = (
     ("A", 0, 0), ("B", 0, 0), ("A", 1, 0), ("B", 1, 0), ("U", 0, 0), ("B", 0, 1), ("c", 0, 0), ("A", 0, 1),
-    ("F", 0, 0), ("B", 1, 1), ("A", 1, 1), ("F", 1, 0), ("B", 0, 2), ("A", 0, 2), ("U", 0, 1), ("B", 1, 2),
-    ("F", 0, 1), ("A", 2, 0), ("A", 1, 2), ("B", 2, 0), ("B", 0, 3), ("F", 1, 1), ("F", 0, 2), ("A", 0, 3),
-    ("n", 0, 0), ("U", 0, 2), ("B", 1, 3), ("A", 1, 3), ("F", 1, 2), ("A", 2, 1), ("B", 0, 4), ("B", 2, 1),
-    ("F", 0, 3), ("A", 0, 4), ("F", 2, 0), ("U", 0, 3), ("B", 1, 4), ("F", 1, 3), ("A", 1, 4), ("A", 3, 0),
-    ("B", 3, 0), ("F", 0, 4), ("G", 0, 0), ("A", 2, 2), ("A", 0, 5), ("B", 2, 2), ("U", 0, 4), ("F", 2, 1),
-    ("A", 1, 5), ("F", 1, 4), ("G", 1, 0), ("B", 3, 1), ("A", 3, 1), ("F", 3, 0), ("G", 0, 1), ("A", 2, 3),
-    ("B", 2, 3), ("U", 0, 5), ("F", 2, 2), ("G", 1, 1), ("B", 3, 2), ("q", 0, 0), ("A", 2, 4), ("B", 2, 4),
-    ("F", 2, 3), ("A", 3, 2), ("F", 3, 1), ("B", 3, 3), ("q", 1, 0), ("F", 3, 2), ("F", 2, 4), ("A", 2, 5),
-    ("G", 2, 0), ("A", 3, 3), ("B", 3, 4), ("t", 0, 1), ("F", 3, 3), ("t", 0, 0), ("G", 2, 1), ("A", 3, 4),
-    ("F", 3, 4), ("G", 3, 0), ("t", 1, 1), ("q", 2, 0), ("A", 3, 5), ("G", 3, 1), ("t", 1, 0), ("t", 2, 1),
-    ("q", 3, 0), ("t", 2, 0), ("t", 3, 1), ("t", 3, 0),
+    ("F", 0, 0), ("B", 1, 1), ("A", 1, 1), ("F", 1, 0), ("B", 0, 2), ("U", 0, 1), ("A", 0, 2), ("B", 1, 2),
+    ("F", 0, 1), ("A", 1, 2), ("F", 1, 1), ("B", 0, 3), ("A", 2, 0), ("B", 2, 0), ("U", 0, 2), ("F", 0, 2),
+    ("n", 0, 0), ("A", 0, 3), ("B", 1, 3), ("F", 1, 2), ("A", 1, 3), ("B", 0, 4), ("B", 2, 1), ("F", 0, 3),
+    ("U", 0, 3), ("A", 3, 0), ("B", 3, 0), ("A", 2, 1), ("A", 0, 4), ("B", 1, 4), ("F", 2, 0), ("A", 1, 4),
+    ("F", 1, 3), ("B", 2, 2), ("U", 0, 4), ("F", 0, 4), ("G", 0, 0), ("B", 3, 1), ("F", 2, 1), ("A", 2, 2),
+    ("A", 3, 1), ("F", 3, 0), ("A", 0, 5), ("F", 1, 4), ("A", 1, 5), ("G", 1, 0), ("U", 0, 5), ("B", 2, 3),
+    ("B", 3, 2), ("G", 0, 1), ("F", 2, 2), ("A", 2, 3), ("F", 3, 1), ("A", 3, 2), ("B", 2, 4), ("G", 1, 1),
+    ("B", 3, 3), ("F", 2, 3), ("q", 0, 0), ("F", 3, 2), ("q", 1, 0), ("A", 2, 4), ("F", 2, 4), ("G", 2, 0),
+    ("A", 3, 3), ("B", 3, 4), ("F", 3, 3), ("t", 0, 1), ("t", 1, 1), ("A", 2, 5), ("G", 2, 1), ("F", 3, 4),
+    ("A", 3, 4), ("G", 3, 0), ("t", 0, 0), ("t", 1, 0), ("A", 3, 5), ("G", 3, 1), ("q", 2, 0), ("t", 2, 1),
+    ("q", 3, 0), ("t", 3, 1), ("t", 2, 0), ("t", 3, 0),
 )
 
 
@@ -236,8 +236,8 @@
             await_token((("A", p), "r", k), (("A", p), "l", k))
         if k < 4:
             ring(("A", p), k, block, 4)
-        for q in offsets(k):
-            push(("A", p, "s", q), W.at[c, :, zat(q), :, cols], sibling, W.at[1 - c, :, zat(q), :, cols])
+        else:
+            push(("A", p, "s"), W.at[c, :, :, :, cols], sibling, W.at[1 - c, :, :, :, cols])
 
     def hand_b(p, i, xo):
         cols = columns_b(p)
@@ -287,7 +287,7 @@
 
     def half_shared(p):
         if SPLIT[p]:
-            await_token(*(("A", p, "s", q) for q in range(-3, 5)))
+            await_token(("A", p, "s"))
         if SPLIT[p] < GROUP:
             await_token(*(("B", p, "s", i) for i in range(4)))
 
@@ -400,12 +400,12 @@
     dma = pltpu.SemaphoreType.DMA
     return pl.pallas_call(
         kernel,
-        out_shape=jax.ShapeDtypeStruct((1, TOK, D), BF16),
+        out_shape=pltpu.VMEM((1, TOK, D), BF16),
         in_specs=[
             anywhere, pl.BlockSpec(memory_space=pltpu.VMEM), anywhere, anywhere, anywhere,
             pl.BlockSpec(memory_space=pltpu.SMEM),
         ],
-        out_specs=anywhere,
+        out_specs=pl.BlockSpec(memory_space=pltpu.VMEM),
         scratch_shapes=[
             pltpu.VMEM((2, NX, NZ, ROWS, 3072), BF16),
             pltpu.VMEM((2, NZ, ROWS, 512), BF16),

time: 91.8 us -> 86.5 us (0.942)
  Pallas kernels: 89.2 us -> 85.3 us
  local copies, waits for them, and re-layouts: 2.3 us -> 0.97 us
    pallas_call x1, Pallas kernels: 89.2 us -> 85.3 us  [per_device(): pl.pallas_call(kernel, out_shape=pltpu.VMEM((1, TOK, D), BF16), in_specs=...]
    unnamed x1, local copies, waits for them, and re-layouts: 2.3 us -> 0.97 us
where the time goes in v3:
time: 86.5 us; the launch traced here: 86.3 us
  Pallas kernels  85.3 us (99%)
  local copies, waits for them, and re-layouts  0.97 us (1%)
    pallas_call x1, Pallas kernels, per_device(): pl.pallas_call(kernel, out_shape=pltpu.VMEM((1, TOK, D), BF16), in_specs=...  85.3 us

profile of v3, /device:TPU:2, one launch (start us, length us, event | category | flops | bytes accessed | tf_op | source)
XLA Modules:
  0.0 86.3 jit_solution(16488312939459882869)
XLA Ops:
  0.0 85.3 %relay_step.1 = bf16[1,256,2048]{2,1,0:T(8,128)(2,1)S(1)} custom-call(bf16[1,256,2048]{2,1,0:T(8,128)(2,1)} %act.1, bf16[1,2048]{1,0:T(2,128)(2,1)} %gain.1, bf16[1,32,2048]{2,1,0:T(8,128)(2,1)} %qw.1, bf16[1,32,1024]{2,1,0:T(8,128)(2,1)} %kvw.1, bf16[1,512,1024]{2,1,0:T(8,128)(2,1)} %cache.1, s32[2,3]{1,0:T(2,128)} %rb.1), custom_call_target="tpu_custom_call" | custom-call | flops 5000000000 | bytes 20000000 | tf_op jit(solution)/shard_map/relay_step/pallas_call | solution.py:401
  85.3 1.0 %copy.8 = bf16[1,256,2048]{2,1,0:T(8,128)(2,1)} copy(bf16[1,256,2048]{2,1,0:T(8,128)(2,1)S(1)} %relay_step.1) | data formatting | bytes 2097152

commit v4 on v3

--- a/solution.py
+++ b/solution.py
@@ -380,9 +380,10 @@
     for name, p, k in ORDER:
         steps[name](p, k)
 
-    await_token(*(("o", j, b) for j in range(KVH) for b in range(2)))
-    for copy in sends:
-        copy.wait_send()
+    late = [i for i, token in enumerate(tokens) if token[0] == "o"]
+    for i, copy in enumerate(sends):
+        if i not in late:
+            copy.wait_send()
     for j in range(KVH):
         pl.when(share < 63)(lambda j=j: halo_copy(j).wait_send())
     pl.when(is_source)(lambda: scatter(lambda copy: copy.wait_send()))
@@ -393,6 +394,9 @@
             trade_copy(k).wait_send()
 
     pl.when(swapped)(traded)
+    await_token(*(("o", j, b) for j in range(KVH) for b in range(2)))
+    for i in late:
+        sends[i].wait_send()
 
 
 def per_device(activations, norm_gain, query_weight, keyval_weight, prefix_cache, random_blocks):

time: 86.5 us -> 86.1 us (level)
  no operation moved by 1% of the time
where the time goes in v4:
time: 86.1 us; the launch traced here: 85.9 us
  Pallas kernels  84.9 us (99%)
  local copies, waits for them, and re-layouts  0.97 us (1%)
    pallas_call x1, Pallas kernels, per_device(): pl.pallas_call(kernel, out_shape=pltpu.VMEM((1, TOK, D), BF16), in_specs=...  84.9 us

profile of v4, /device:TPU:2, one launch (start us, length us, event | category | flops | bytes accessed | tf_op | source)
XLA Modules:
  0.0 85.9 jit_solution(16578428364818498460)
XLA Ops:
  0.0 84.9 %relay_step.1 = bf16[1,256,2048]{2,1,0:T(8,128)(2,1)S(1)} custom-call(bf16[1,256,2048]{2,1,0:T(8,128)(2,1)} %act.1, bf16[1,2048]{1,0:T(2,128)(2,1)} %gain.1, bf16[1,32,2048]{2,1,0:T(8,128)(2,1)} %qw.1, bf16[1,32,1024]{2,1,0:T(8,128)(2,1)} %kvw.1, bf16[1,512,1024]{2,1,0:T(8,128)(2,1)} %cache.1, s32[2,3]{1,0:T(2,128)} %rb.1), custom_call_target="tpu_custom_call" | custom-call | flops 5000000000 | bytes 20000000 | tf_op jit(solution)/shard_map/relay_step/pallas_call | solution.py:405
  84.9 1.0 %copy.8 = bf16[1,256,2048]{2,1,0:T(8,128)(2,1)} copy(bf16[1,256,2048]{2,1,0:T(8,128)(2,1)S(1)} %relay_step.1) | data formatting | bytes 2097152

commit v5 on v4

--- a/solution.py
+++ b/solution.py
@@ -20,21 +20,21 @@
 SCALE = math.log2(math.e) / math.sqrt(HD)
 
 GROUP = 768
-SPLIT = (256, 256, 384, 128)
+SPLIT = (256, 256, 256, 256)
 NTOKENS = 217
 ORDER = (
     ("A", 0, 0), ("B", 0, 0), ("A", 1, 0), ("B", 1, 0), ("U", 0, 0), ("B", 0, 1), ("c", 0, 0), ("A", 0, 1),
     ("F", 0, 0), ("B", 1, 1), ("A", 1, 1), ("F", 1, 0), ("B", 0, 2), ("U", 0, 1), ("A", 0, 2), ("B", 1, 2),
     ("F", 0, 1), ("A", 1, 2), ("F", 1, 1), ("B", 0, 3), ("A", 2, 0), ("B", 2, 0), ("U", 0, 2), ("F", 0, 2),
-    ("n", 0, 0), ("A", 0, 3), ("B", 1, 3), ("F", 1, 2), ("A", 1, 3), ("B", 0, 4), ("B", 2, 1), ("F", 0, 3),
-    ("U", 0, 3), ("A", 3, 0), ("B", 3, 0), ("A", 2, 1), ("A", 0, 4), ("B", 1, 4), ("F", 2, 0), ("A", 1, 4),
-    ("F", 1, 3), ("B", 2, 2), ("U", 0, 4), ("F", 0, 4), ("G", 0, 0), ("B", 3, 1), ("F", 2, 1), ("A", 2, 2),
-    ("A", 3, 1), ("F", 3, 0), ("A", 0, 5), ("F", 1, 4), ("A", 1, 5), ("G", 1, 0), ("U", 0, 5), ("B", 2, 3),
-    ("B", 3, 2), ("G", 0, 1), ("F", 2, 2), ("A", 2, 3), ("F", 3, 1), ("A", 3, 2), ("B", 2, 4), ("G", 1, 1),
-    ("B", 3, 3), ("F", 2, 3), ("q", 0, 0), ("F", 3, 2), ("q", 1, 0), ("A", 2, 4), ("F", 2, 4), ("G", 2, 0),
-    ("A", 3, 3), ("B", 3, 4), ("F", 3, 3), ("t", 0, 1), ("t", 1, 1), ("A", 2, 5), ("G", 2, 1), ("F", 3, 4),
-    ("A", 3, 4), ("G", 3, 0), ("t", 0, 0), ("t", 1, 0), ("A", 3, 5), ("G", 3, 1), ("q", 2, 0), ("t", 2, 1),
-    ("q", 3, 0), ("t", 3, 1), ("t", 2, 0), ("t", 3, 0),
+    ("n", 0, 0), ("A", 0, 3), ("B", 1, 3), ("F", 1, 2), ("A", 1, 3), ("B", 0, 4), ("A", 3, 0), ("F", 0, 3),
+    ("B", 2, 1), ("U", 0, 3), ("B", 3, 0), ("A", 2, 1), ("F", 2, 0), ("A", 0, 4), ("B", 1, 4), ("F", 1, 3),
+    ("A", 1, 4), ("B", 2, 2), ("F", 0, 4), ("G", 0, 0), ("U", 0, 4), ("B", 3, 1), ("A", 3, 1), ("A", 2, 2),
+    ("A", 0, 5), ("F", 2, 1), ("A", 1, 5), ("F", 3, 0), ("B", 2, 3), ("U", 0, 5), ("F", 1, 4), ("G", 1, 0),
+    ("B", 3, 2), ("A", 3, 2), ("F", 2, 2), ("G", 0, 1), ("A", 2, 3), ("B", 2, 4), ("F", 3, 1), ("B", 3, 3),
+    ("q", 0, 0), ("G", 1, 1), ("F", 2, 3), ("A", 2, 4), ("A", 3, 3), ("F", 3, 2), ("B", 3, 4), ("t", 0, 1),
+    ("q", 1, 0), ("A", 2, 5), ("F", 2, 4), ("G", 2, 0), ("F", 3, 3), ("A", 3, 4), ("F", 3, 4), ("G", 3, 0),
+    ("t", 1, 1), ("G", 2, 1), ("t", 0, 0), ("A", 3, 5), ("G", 3, 1), ("q", 2, 0), ("t", 1, 0), ("q", 3, 0),
+    ("t", 2, 1), ("t", 3, 1), ("t", 2, 0), ("t", 3, 0),
 )
 
 

time: 86.1 us -> 87.1 us (1.012)
  Pallas kernels: 84.9 us -> 86 us
    pallas_call x1, Pallas kernels: 84.9 us -> 86 us  [per_device(): pl.pallas_call(kernel, out_shape=pltpu.VMEM((1, TOK, D), BF16), in_specs=...]
where the time goes in v5:
time: 87.1 us; the launch traced here: 87 us
  Pallas kernels  86 us (99%)
  local copies, waits for them, and re-layouts  0.97 us (1%)
    pallas_call x1, Pallas kernels, per_device(): pl.pallas_call(kernel, out_shape=pltpu.VMEM((1, TOK, D), BF16), in_specs=...  86 us

profile of v5, /device:TPU:2, one launch (start us, length us, event | category | flops | bytes accessed | tf_op | source)
XLA Modules:
  0.0 87.0 jit_solution(11209960903382938945)
XLA Ops:
  0.0 86.0 %relay_step.1 = bf16[1,256,2048]{2,1,0:T(8,128)(2,1)S(1)} custom-call(bf16[1,256,2048]{2,1,0:T(8,128)(2,1)} %act.1, bf16[1,2048]{1,0:T(2,128)(2,1)} %gain.1, bf16[1,32,2048]{2,1,0:T(8,128)(2,1)} %qw.1, bf16[1,32,1024]{2,1,0:T(8,128)(2,1)} %kvw.1, bf16[1,512,1024]{2,1,0:T(8,128)(2,1)} %cache.1, s32[2,3]{1,0:T(2,128)} %rb.1), custom_call_target="tpu_custom_call" | custom-call | flops 5000000000 | bytes 20000000 | tf_op jit(solution)/shard_map/relay_step/pallas_call | solution.py:405
  86.0 1.0 %copy.8 = bf16[1,256,2048]{2,1,0:T(8,128)(2,1)} copy(bf16[1,256,2048]{2,1,0:T(8,128)(2,1)S(1)} %relay_step.1) | data formatting | bytes 2097152
